TPU v7x, 32 devices: a whole 2x2x4 slice. The times are simulated.
32 devices in a mesh: rep: 8 (over z, x), fsdp: 4 (over y, core).
Axes of the slice: x: 2, y: 2, z: 4, core: 2. Of those that a mesh axis runs over, the one named last changes fastest.
Arguments:
- activations: bfloat16 [8, 768, 4096], P('rep', 'fsdp'), may hold values from -6 to 6
- weights: float32 [8, 4096, 512], P('rep', 'fsdp'), may hold values from -6 to 6
- cotangent: bfloat16 [8, 768, 512], P('rep', 'fsdp'), may hold values from -6 to 6
- step_index: int32 [1], replicated, may hold values from 0 to 999
Outputs:
- projected: bfloat16 [8, 768, 512], P('rep', 'fsdp')
- input_grad: bfloat16 [8, 768, 4096], P('rep', 'fsdp')
- mixed: float32 [8, 4096, 512], P('rep', 'fsdp')
All inputs are finite; a program needn't handle non-finite values.
Results may differ from a plain program's by a relative error of at most 0.005.
Values may be sent and summed in bfloat16 or wider, within the bound.
A program may use at most 64 MiB of HBM per device.

v0:
```python
import functools

import jax
import jax.numpy as jnp
from jax import lax
from jax.experimental import pallas as pl
from jax.experimental.pallas import tpu as pltpu
from jax.sharding import PartitionSpec as P

BITS = 3
MESH = pl.DeviceIdType.MESH
BF16 = jnp.bfloat16
F32 = jnp.float32


def kernel(
    bit, chips, chunks, scale,
    step_ref, act_hbm, w_hbm, cot_hbm,
    proj_ref, ig_ref, mixed_ref,
    act, cot, w, wb, ig, part, to_sib, from_sib, to_chip, from_chip, give, take,
    local_sem, cot_send, cot_recv, act_send, act_recv, ig_send, ig_recv,
    sib_send, sib_recv, chip_send, chip_recv, give_sem, take_sem,
):
    rep, me = lax.axis_index("rep"), lax.axis_index("fsdp")
    chip, core = me // 2, me % 2
    tokens = cot_hbm.shape[1]
    rows = w_hbm.shape[1]
    slots = 2 * chips
    half = 2 ** bit
    partner = rep + half - 2 * half * ((rep // half) % 2)

    def device(ahead, other):
        return ((chip + ahead + chips) % chips) * 2 + (core + other) % 2

    def sender(slot):
        return device(-(slot // 2), slot % 2)

    def receiver(slot):
        return device(slot // 2, slot % 2)

    def to_peer(src, dst, send, recv, peer):
        return pltpu.make_async_remote_copy(
            src_ref=src, dst_ref=dst, send_sem=send, recv_sem=recv,
            device_id=(rep, peer), device_id_type=MESH,
        )

    def of(slot):
        return pl.ds(slot * tokens, tokens)

    def cols(owner):
        return pl.ds(pl.multiple_of(owner * rows, rows), rows)

    def piece(owner, c):
        start, size = chunks[c].start, chunks[c].size
        return pl.ds(pl.multiple_of(owner * rows + start, 128), size)

    load_cot = pltpu.make_async_copy(cot_hbm.at[0], cot.at[of(0)], local_sem.at[0])
    load_act = pltpu.make_async_copy(act_hbm.at[0, :, cols(me)], act.at[of(0)], local_sem.at[1])
    load_w = pltpu.make_async_copy(w_hbm.at[0], w, local_sem.at[2])
    load_cot.start()
    load_w.start()
    load_act.start()

    barrier = pltpu.get_barrier_semaphore()
    for slot in range(1, slots):
        pl.semaphore_signal(barrier, inc=1, device_id=(rep, receiver(slot)), device_id_type=MESH)
    pl.semaphore_signal(barrier, inc=1, device_id=(partner, me), device_id_type=MESH)
    pl.semaphore_wait(barrier, slots)

    far = list(range(2, slots))
    order = far + [1]
    width = w.shape[1]
    halves = [pl.ds(0, width // 2), pl.ds(width // 2, width // 2)]
    cot_copies, act_copies, ig_copies = {}, {}, {}

    def start_cot(h, src, slot, peer):
        copy = to_peer(
            src, cot.at[of(slot), halves[h]],
            cot_send.at[h * slots + slot], cot_recv.at[h * slots + slot], peer)
        copy.start()
        cot_copies[h, slot] = copy

    def send_cot(h):
        for slot in list(range(2, slots, 2)) + [1]:
            start_cot(h, cot_hbm.at[0, :, halves[h]], slot, receiver(slot))

    def take_cot(h):
        for slot in range(2, slots, 2):
            cot_copies[h, slot].wait_recv()
            start_cot(h, cot.at[of(slot), halves[h]], slot + 1, device(0, 1))

    def wait_cot(h):
        for slot in range(1, slots, 2):
            cot_copies[h, slot].wait_recv()

    def send_act(c):
        for slot in order:
            copy = to_peer(
                act_hbm.at[0, :, piece(receiver(slot), c)],
                act.at[of(slot), chunks[c]],
                act_send.at[c * slots + slot], act_recv.at[c * slots + slot], receiver(slot))
            copy.start()
            act_copies[c, slot] = copy

    def wait_act(c):
        for slot in order:
            act_copies[c, slot].wait_recv()

    def input_grad(slot):
        grad = (lax.dot_general(
            cot[of(slot), :], wb[...], (((1,), (1,)), ((), ())), preferred_element_type=F32
        ) * scale).astype(BF16)
        if slot == 0:
            ig_ref[0, :, cols(me)] = grad
        else:
            ig[of(slot - 1), :] = grad

    def send_ig(slot):
        copy = to_peer(
            ig.at[of(slot - 1)], ig_ref.at[0, :, cols(me)], ig_send.at[slot], ig_recv.at[slot], sender(slot))
        copy.start()
        ig_copies[slot] = copy

    later = [functools.partial(send_act, c) for c in range(1, len(chunks))]

    def send_next(most=1):
        for _ in range(most):
            if later:
                later.pop(0)()

    gossip = []

    def update(here, across):
        grad = lax.dot_general(
            act[:, here], cot[:, across], (((0,), (0,)), ((), ())), preferred_element_type=F32)
        new = w[here, across] - rate[:, across.start:across.start + across.size] * (grad * scale)
        mixed_ref[0, here, across] = new
        give[here, across] = new.astype(BF16)
        at = len(gossip)
        copy = pltpu.make_async_remote_copy(
            src_ref=give.at[here, across], dst_ref=take.at[here, across],
            send_sem=give_sem.at[at], recv_sem=take_sem.at[at],
            device_id=(partner, me), device_id_type=MESH,
        )
        copy.start()
        gossip.append((here, across, copy))

    def project(c):
        here = chunks[c]
        for slot in range(slots):
            term = lax.dot_general(
                act[of(slot), here], wb[here, :], (((1,), (0,)), ((), ())), preferred_element_type=F32)
            part[of(slot), :] = term if c == 0 else part[of(slot), :] + term

    send_cot(0)
    send_act(0)
    send_cot(1)

    step = jnp.full((1, width), step_ref[0], jnp.int32).astype(F32)
    rate = 0.3 / jnp.sqrt(1.0 + step / 50.0)
    load_w.wait()
    load_cot.wait()
    load_act.wait()

    take_cot(0)
    send_next()
    wait_cot(0)
    wait_act(0)
    send_next()
    update(chunks[0], halves[0])
    take_cot(1)
    send_next()
    wb[...] = w[...].astype(BF16)
    wait_cot(1)
    update(chunks[0], halves[1])

    for c in range(1, len(chunks)):
        wait_act(c)
        send_next()
        update(chunks[c], pl.ds(0, width))
        if c == 1:
            for slot in order + [0]:
                input_grad(slot)
            send_ig(1)
            later += [functools.partial(send_ig, slot) for slot in far]
            project(0)
        project(c)
    send_next(len(later))

    sib_copies = []
    for ahead in list(range(1, chips)) + [0]:
        here = pl.ds(ahead * tokens, tokens)
        to_sib[here, :] = part[of(2 * ahead + 1), :].astype(BF16)
        copy = to_peer(
            to_sib.at[here], from_sib.at[here], sib_send.at[ahead], sib_recv.at[ahead], device(0, 1))
        copy.start()
        sib_copies.append((ahead, copy))
    chip_copies = []
    for ahead, copy in sib_copies:
        here = pl.ds(ahead * tokens, tokens)
        copy.wait_recv()
        if ahead > 0:
            to_chip[here, :] = (part[of(2 * ahead), :] + from_sib[here, :].astype(F32)).astype(BF16)
            on = to_peer(
                to_chip.at[here], from_chip.at[here], chip_send.at[ahead], chip_recv.at[ahead], sender(2 * ahead))
            on.start()
            chip_copies.append((ahead, on))

    for here, across, copy in gossip:
        copy.wait_recv()
        mixed_ref[0, here, across] = 0.5 * (mixed_ref[0, here, across] + take[here, across].astype(F32))

    total = part[of(0), :] + from_sib[pl.ds(0, tokens), :].astype(F32)
    for ahead, on in chip_copies:
        on.wait_recv()
        total = total + from_chip[pl.ds(ahead * tokens, tokens), :].astype(F32)
    proj_ref[0] = (total * scale).astype(BF16)

    for copy in ig_copies.values():
        copy.wait_recv()
    for copy in list(cot_copies.values()) + list(act_copies.values()) + list(ig_copies.values()):
        copy.wait_send()
    for copy in [copy for _, copy in sib_copies + chip_copies] + [copy for _, _, copy in gossip]:
        copy.wait_send()


def store_kernel(proj_ref, ig_ref, mixed_ref, proj_hbm, ig_hbm, mixed_hbm, sem):
    copies = [pltpu.make_async_copy(proj_ref, proj_hbm, sem.at[0])]
    for src, dst in ((ig_ref, ig_hbm), (mixed_ref, mixed_hbm)):
        size = src.shape[1] // 4
        for c in range(4):
            here = pl.ds(c * size, size)
            copies.append(pltpu.make_async_copy(src.at[0, here], dst.at[0, here], sem.at[len(copies)]))
    for copy in copies:
        copy.start()
    for copy in copies:
        copy.wait()


def step_kernel(bit, count, activations, weights, cotangent, step_index):
    tokens, features = activations.shape[1:]
    rows, width = weights.shape[1:]
    chips = count // 2
    chunks = [pl.ds(start, 128) for start in range(0, min(rows, 256), 128)]
    chunks += [pl.ds(start, 256) for start in range(256, rows, 256)]
    pieces = len(chunks) + 1
    every = count * tokens
    dma = pltpu.SemaphoreType.DMA
    anywhere = pl.BlockSpec(memory_space=pl.ANY)
    in_vmem = pl.BlockSpec(memory_space=pltpu.VMEM)
    results = pl.pallas_call(
        functools.partial(kernel, bit, chips, chunks, features ** (-0.5)),
        out_shape=(
            pltpu.VMEM((1, tokens, width), BF16),
            pltpu.VMEM((1, tokens, features), BF16),
            pltpu.VMEM((1, rows, width), F32),
        ),
        in_specs=[pl.BlockSpec(memory_space=pltpu.SMEM), anywhere, anywhere, anywhere],
        out_specs=(in_vmem, in_vmem, in_vmem),
        scratch_shapes=[
            pltpu.VMEM((every, rows), BF16),
            pltpu.VMEM((every, width), BF16),
            pltpu.VMEM((rows, width), F32),
            pltpu.VMEM((rows, width), BF16),
            pltpu.VMEM((every - tokens, rows), BF16),
            pltpu.VMEM((every, width), F32),
            pltpu.VMEM((chips * tokens, width), BF16),
            pltpu.VMEM((chips * tokens, width), BF16),
            pltpu.VMEM((chips * tokens, width), BF16),
            pltpu.VMEM((chips * tokens, width), BF16),
            pltpu.VMEM((rows, width), BF16),
            pltpu.VMEM((rows, width), BF16),
            dma((3,)),
            dma((2 * count,)), dma((2 * count,)),
            dma((len(chunks) * count,)), dma((len(chunks) * count,)),
            dma((count,)), dma((count,)),
            dma((chips,)), dma((chips,)),
            dma((chips,)), dma((chips,)),
            dma((pieces,)), dma((pieces,)),
        ],
        compiler_params=pltpu.CompilerParams(
            collective_id=bit, has_side_effects=True, vmem_limit_bytes=40 * 2 ** 20),
        cost_estimate=pl.CostEstimate(
            flops=6 * every * rows * width, bytes_accessed=8 * 2 ** 20, transcendentals=0),
        name="step_bit_%d" % bit,
    )(step_index, activations, weights, cotangent)
    return pl.pallas_call(
        store_kernel,
        out_shape=tuple(jax.ShapeDtypeStruct(part.shape, part.dtype) for part in results),
        in_specs=[anywhere] * 3,
        out_specs=(anywhere, anywhere, anywhere),
        scratch_shapes=[dma((9,))],
        compiler_params=pltpu.CompilerParams(vmem_limit_bytes=2 ** 20),
        name="store",
    )(*results)


def body(count, activations, weights, cotangent, step_index):
    branches = [functools.partial(step_kernel, bit, count) for bit in range(BITS)]
    return lax.switch(step_index[0] % BITS, branches, activations, weights, cotangent, step_index)


def solution(mesh):
    split = P("rep", "fsdp", None)
    return jax.shard_map(
        functools.partial(body, mesh.shape["fsdp"]),
        mesh=mesh,
        in_specs=(split, split, split, P()),
        out_specs=(split, split, split),
        check_vma=False,
    )
```

profile of v0, /device:TPU:0, one launch (start us, length us, event | category | flops | bytes accessed | tf_op | source)
XLA Modules:
  0.0 52.5 jit_solution(12375057127921308223)
XLA Ops:
  1.3 51.0 %conditional.1 = ((bf16[1,192,512]{2,1,0:T(8,128)(2,1)}, bf16[1,192,4096]{2,1,0:T(8,128)(2,1)}, f32[1,1024,512]{2,1,0:T(8,128)})) conditional(s32[]{:T(128)} %clamp.3, (s32[1]{0:T(128)}, bf16[1,192,4096]{2,1,0:T(8,128)(2,1)}, f32[1,1024,512]{2,1,0:T(8,128)}, bf16[1,192,512]{2,1,0:T(8,128)(2,1)}) %tuple.16, (s32[1]{0:T(128)}, ...), branch_computations={%region_0.1_spmd, %region_1.2_spmd, %region_2.3_spmd} | conditional | flops 2415919104 | bytes 8388616 | solution.py:300
  1.3 48.8 %step_bit_0.1 = (bf16[1,192,512]{2,1,0:T(8,128)(2,1)S(1)}, bf16[1,192,4096]{2,1,0:T(8,128)(2,1)S(1)}, f32[1,1024,512]{2,1,0:T(8,128)S(1)}) custom-call(s32[1]{0:T(128)} %get-tuple-element.24.step_ref, bf16[1,192,4096]{2,1,0:T(8,128)(2,1)} %get-tuple-element.69.act_hbm, f32[1,1024,512]{2,1,0:T(8,128)} %get-tuple-element.72.w_hbm, ...), custom_call_target="tpu_custom_call" | custom-call | flops 2415919104 | bytes 8388608 | tf_op jit(solution)/shard_map/cond/branch_0_fun/step_bit_0/pallas_call | solution.py:251
  50.1 2.0 %store.3 = (bf16[1,192,512]{2,1,0:T(8,128)(2,1)}, bf16[1,192,4096]{2,1,0:T(8,128)(2,1)}, f32[1,1024,512]{2,1,0:T(8,128)}) custom-call(bf16[1,192,512]{2,1,0:T(8,128)(2,1)S(1)} %get-tuple-element.28.proj_ref, bf16[1,192,4096]{2,1,0:T(8,128)(2,1)S(1)} %get-tuple-element.29.ig_ref, f32[1,1024,512]{2,1,0:T(8,128)S(1)} %get-tuple-element.30.mixed_ref), custom_call_target="tpu_custom_call" | custom-call | tf_op jit(solution)/shard_map/cond/branch_0_fun/store/pallas_call | solution.py:287
where the time goes:
time: 52.7 us; the launch traced here: 52.5 us
  Pallas kernels  50.8 us (96%)
  between operations  1.47 us (3%)
    pallas_call x1, Pallas kernels, step_kernel(): pl.pallas_call(functools.partial(kernel, bit, chips, chunks, features **...  48.8 us
    pallas_call x1, Pallas kernels, step_kernel(): pl.pallas_call(store_kernel, out_shape=tuple((jax.ShapeDtypeStruct(part.s...  1.97 us

commit v1 on v0

--- a/solution.py
+++ b/solution.py
@@ -224,6 +224,174 @@
         copy.wait_send()
 
 
+def pair_kernel(
+    bit, half_rows, scale,
+    step_ref, act_hbm, w_hbm, cot_hbm,
+    proj_ref, ig_ref, mixed_ref,
+    act, cot, w, ws, acc, p_out, p_in, q, pair_out, pair_in, w_in, s_out, s_in,
+    plain_out, plain_in, new_out, new_in, back_out, back_in,
+    local_sem, ws_send, ws_recv, p_send, p_recv, far_send, far_recv, pair_send, pair_recv,
+):
+    rep, me = lax.axis_index("rep"), lax.axis_index("fsdp")
+    chip, core = me // 2, me % 2
+    owners = [me, chip * 2 + 1 - core, (1 - chip) * 2 + core, (1 - chip) * 2 + 1 - core]
+    rows, width = w.shape
+    size = rows // 4
+    sub = half_rows // 2
+    plain = pl.ds(2 * half_rows, rows - 2 * half_rows)
+    side = (rep // 2 ** bit) % 2
+    partner = rep + 2 ** bit - 2 * 2 ** bit * side
+    mine, theirs = side * half_rows, (1 - side) * half_rows
+    started = []
+
+    def go(src, dst, send, recv, at, device):
+        copy = pltpu.make_async_remote_copy(
+            src_ref=src, dst_ref=dst, send_sem=send.at[at], recv_sem=recv.at[at],
+            device_id=device, device_id_type=MESH,
+        )
+        copy.start()
+        started.append(copy)
+        return copy
+
+    core_id, far_id, pair_id = (rep, owners[1]), (rep, owners[2]), (partner, me)
+
+    def part(start, count):
+        return pl.ds(pl.multiple_of(start, 16), count)
+
+    def lanes(slot, k):
+        return pl.ds(pl.multiple_of(owners[slot] * rows + k * size, 128), size)
+
+    load_w = pltpu.make_async_copy(w_hbm.at[0], w, local_sem.at[0])
+    load_cot = pltpu.make_async_copy(cot_hbm.at[0], cot, local_sem.at[1])
+    load_act = pltpu.make_async_copy(act_hbm.at[0], act, local_sem.at[2])
+    load_w.start()
+    load_cot.start()
+    load_act.start()
+
+    barrier = pltpu.get_barrier_semaphore()
+    for device in (core_id, far_id, pair_id):
+        pl.semaphore_signal(barrier, inc=1, device_id=device, device_id_type=MESH)
+    load_w.wait()
+    ws[pl.ds(0, rows), :] = w[...].astype(BF16)
+    pl.semaphore_wait(barrier, 3)
+
+    def send_w(slot, k):
+        source = 2 if slot == 3 else 0
+        return go(
+            ws.at[pl.ds(source * rows + k * size, size)], ws.at[pl.ds(slot * rows + k * size, size)],
+            ws_send, ws_recv, slot * 4 + k, far_id if slot == 2 else core_id)
+
+    w_copies = {(2, k): send_w(2, k) for k in (0, 1)}
+    w_pair = go(ws.at[part(theirs, half_rows)], w_in, pair_send, pair_recv, 0, pair_id)
+    load_cot.wait()
+    load_act.wait()
+
+    def term(slot, k):
+        return lax.dot_general(
+            act[:, lanes(slot, k)], cot[...], (((0,), (0,)), ((), ())), preferred_element_type=F32)
+
+    p_copies = {}
+    for k in range(4):
+        for at, slot in ((1, 3), (0, 1)):
+            here = pl.ds(at * rows + k * size, size)
+            p_out[here, :] = term(slot, k).astype(BF16)
+            p_copies[at, k] = go(p_out.at[here], p_in.at[here], p_send, p_recv, at * 4 + k, core_id)
+    for k in range(4):
+        w_copies[1, k] = send_w(1, k)
+    for k in range(4):
+        for at, slot in ((1, 2), (0, 0)):
+            here = pl.ds(at * rows + k * size, size)
+            own = term(slot, k)
+            p_copies[at, k].wait_recv()
+            q[here, :] = own + p_in[here, :].astype(F32)
+
+    pair_copies = {}
+    for at in (1, 0):
+        for j in range(2):
+            here = pl.ds(at * half_rows + j * sub, sub)
+            pair_out[here, :] = q[part(at * rows + theirs + j * sub, sub), :].astype(BF16)
+            pair_copies[at, j] = go(
+                pair_out.at[here], pair_in.at[here], pair_send, pair_recv, 1 + at * 2 + j, pair_id)
+    plain_out[...] = q[pl.ds(rows + 2 * half_rows, rows - 2 * half_rows), :].astype(BF16)
+    plain_copy = go(plain_out, plain_in, far_send, far_recv, 0, far_id)
+
+    step = jnp.full((1, width), step_ref[0], jnp.int32).astype(F32)
+    rate = 0.3 / jnp.sqrt(1.0 + step / 50.0) * scale
+
+    def multiply(slot, k):
+        block = ws[pl.ds(slot * rows + k * size, size), :]
+        ig_ref[0, :, lanes(slot, k)] = (lax.dot_general(
+            cot[...], block, (((1,), (1,)), ((), ())), preferred_element_type=F32) * scale).astype(BF16)
+        out = jnp.dot(act[:, lanes(slot, k)], block, preferred_element_type=F32)
+        acc[...] = out if (slot, k) == (0, 0) else acc[...] + out
+
+    def arrive(k):
+        w_copies[2, k].wait_recv()
+        w_copies[3, k] = send_w(3, k)
+
+    for k in range(4):
+        multiply(0, k)
+    arrive(0)
+    w_copies[2, 2] = send_w(2, 2)
+    for k in range(4):
+        w_copies[1, k].wait_recv()
+        multiply(1, k)
+
+    far_copies = []
+    for j in range(2):
+        here = pl.ds(j * sub, sub)
+        pair_copies[1, j].wait_recv()
+        s_out[here, :] = (
+            q[part(rows + mine + j * sub, sub), :] + pair_in[pl.ds(half_rows + j * sub, sub), :].astype(F32)
+        ).astype(BF16)
+        far_copies.append(go(s_out.at[here], s_in.at[here], far_send, far_recv, 1 + j, far_id))
+
+    arrive(1)
+    w_copies[2, 3] = send_w(2, 3)
+    multiply(2, 0)
+    multiply(2, 1)
+
+    plain_copy.wait_recv()
+    new = w[plain, :] - rate * (q[plain, :] + plain_in[...].astype(F32))
+    mixed_ref[0, plain, :] = new
+    new_out[...] = new.astype(BF16)
+    new_copy = go(new_out, new_in, pair_send, pair_recv, 5, pair_id)
+
+    w_pair.wait_recv()
+    back_copies = []
+    for j in range(2):
+        here = pl.ds(j * sub, sub)
+        there = part(mine + j * sub, sub)
+        pair_copies[0, j].wait_recv()
+        far_copies[j].wait_recv()
+        grad = (q[there, :] + pair_in[here, :].astype(F32)) + s_in[here, :].astype(F32)
+        mean = 0.5 * ((w[there, :] + w_in[here, :].astype(F32)) - rate * grad)
+        mixed_ref[0, there, :] = mean
+        back_out[here, :] = mean.astype(BF16)
+        back_copies.append(go(back_out.at[here], back_in.at[here], pair_send, pair_recv, 6 + j, pair_id))
+
+    arrive(2)
+    multiply(2, 2)
+    for k in (0, 1):
+        w_copies[3, k].wait_recv()
+        multiply(3, k)
+    arrive(3)
+    multiply(2, 3)
+    w_copies[3, 2].wait_recv()
+    multiply(3, 2)
+
+    new_copy.wait_recv()
+    mixed_ref[0, plain, :] = 0.5 * (mixed_ref[0, plain, :] + new_in[...].astype(F32))
+    w_copies[3, 3].wait_recv()
+    multiply(3, 3)
+    proj_ref[0] = (acc[...] * scale).astype(BF16)
+    for j in range(2):
+        back_copies[j].wait_recv()
+        mixed_ref[0, part(theirs + j * sub, sub), :] = back_in[pl.ds(j * sub, sub), :].astype(F32)
+    for copy in started:
+        copy.wait_send()
+
+
 def store_kernel(proj_ref, ig_ref, mixed_ref, proj_hbm, ig_hbm, mixed_hbm, sem):
     copies = [pltpu.make_async_copy(proj_ref, proj_hbm, sem.at[0])]
     for src, dst in ((ig_ref, ig_hbm), (mixed_ref, mixed_hbm)):
@@ -248,16 +416,28 @@
     dma = pltpu.SemaphoreType.DMA
     anywhere = pl.BlockSpec(memory_space=pl.ANY)
     in_vmem = pl.BlockSpec(memory_space=pltpu.VMEM)
-    results = pl.pallas_call(
-        functools.partial(kernel, bit, chips, chunks, features ** (-0.5)),
-        out_shape=(
-            pltpu.VMEM((1, tokens, width), BF16),
-            pltpu.VMEM((1, tokens, features), BF16),
-            pltpu.VMEM((1, rows, width), F32),
-        ),
-        in_specs=[pl.BlockSpec(memory_space=pltpu.SMEM), anywhere, anywhere, anywhere],
-        out_specs=(in_vmem, in_vmem, in_vmem),
-        scratch_shapes=[
+    half_rows = rows * 5 // 16
+    if chips == 2 and bit < 2 and rows % 1024 == 0:
+        run = functools.partial(pair_kernel, bit, half_rows, features ** (-0.5))
+
+        def block(count):
+            return pltpu.VMEM((count, width), BF16)
+
+        scratch = [
+            pltpu.VMEM((tokens, features), BF16), block(tokens),
+            pltpu.VMEM((rows, width), F32), block(4 * rows), pltpu.VMEM((tokens, width), F32),
+            block(2 * rows), block(2 * rows), pltpu.VMEM((2 * rows, width), F32),
+            block(2 * half_rows), block(2 * half_rows), block(half_rows),
+            block(half_rows), block(half_rows),
+            block(rows - 2 * half_rows), block(rows - 2 * half_rows),
+            block(rows - 2 * half_rows), block(rows - 2 * half_rows),
+            block(half_rows), block(half_rows),
+            dma((3,)), dma((16,)), dma((16,)), dma((8,)), dma((8,)),
+            dma((3,)), dma((3,)), dma((8,)), dma((8,)),
+        ]
+    else:
+        run = functools.partial(kernel, bit, chips, chunks, features ** (-0.5))
+        scratch = [
             pltpu.VMEM((every, rows), BF16),
             pltpu.VMEM((every, width), BF16),
             pltpu.VMEM((rows, width), F32),
@@ -277,7 +457,17 @@
             dma((chips,)), dma((chips,)),
             dma((chips,)), dma((chips,)),
             dma((pieces,)), dma((pieces,)),
-        ],
+        ]
+    results = pl.pallas_call(
+        run,
+        out_shape=(
+            pltpu.VMEM((1, tokens, width), BF16),
+            pltpu.VMEM((1, tokens, features), BF16),
+            pltpu.VMEM((1, rows, width), F32),
+        ),
+        in_specs=[pl.BlockSpec(memory_space=pltpu.SMEM), anywhere, anywhere, anywhere],
+        out_specs=(in_vmem, in_vmem, in_vmem),
+        scratch_shapes=scratch,
         compiler_params=pltpu.CompilerParams(
             collective_id=bit, has_side_effects=True, vmem_limit_bytes=40 * 2 ** 20),
         cost_estimate=pl.CostEstimate(

time: 52.7 us -> 50.1 us (0.951)
  Pallas kernels: 50.8 us -> 47.7 us
    pallas_call x1, Pallas kernels: 48.8 us -> 45.7 us  [step_kernel(): pl.pallas_call(run, out_shape=(pltpu.VMEM((1, tokens, width), BF16), pltp...]
where the time goes in v1:
time: 50.1 us; the launch traced here: 49.6 us
  Pallas kernels  47.7 us (95%)
  between operations  1.47 us (3%)
    pallas_call x1, Pallas kernels, step_kernel(): pl.pallas_call(run, out_shape=(pltpu.VMEM((1, tokens, width), BF16), pltp...  45.7 us
    pallas_call x1, Pallas kernels, step_kernel(): pl.pallas_call(store_kernel, out_shape=tuple((jax.ShapeDtypeStruct(part.s...  1.97 us

profile of v1, /device:TPU:0, one launch (start us, length us, event | category | flops | bytes accessed | tf_op | source)
XLA Modules:
  0.0 49.6 jit_solution(428501002508102414)
XLA Ops:
  1.3 48.2 %conditional.1 = ((bf16[1,192,512]{2,1,0:T(8,128)(2,1)}, bf16[1,192,4096]{2,1,0:T(8,128)(2,1)}, f32[1,1024,512]{2,1,0:T(8,128)})) conditional(s32[]{:T(128)} %clamp.3, (s32[1]{0:T(128)}, bf16[1,192,4096]{2,1,0:T(8,128)(2,1)}, f32[1,1024,512]{2,1,0:T(8,128)}, bf16[1,192,512]{2,1,0:T(8,128)(2,1)}) %tuple.16, (s32[1]{0:T(128)}, ...), branch_computations={%region_0.1_spmd, %region_1.2_spmd, %region_2.3_spmd} | conditional | flops 2415919104 | bytes 8388616 | solution.py:490
  1.3 45.7 %step_bit_1.1 = (bf16[1,192,512]{2,1,0:T(8,128)(2,1)S(1)}, bf16[1,192,4096]{2,1,0:T(8,128)(2,1)S(1)}, f32[1,1024,512]{2,1,0:T(8,128)S(1)}) custom-call(s32[1]{0:T(128)} %get-tuple-element.31.step_ref, bf16[1,192,4096]{2,1,0:T(8,128)(2,1)} %get-tuple-element.70.act_hbm, f32[1,1024,512]{2,1,0:T(8,128)} %get-tuple-element.73.w_hbm, ...), custom_call_target="tpu_custom_call" | custom-call | flops 2415919104 | bytes 8388608 | tf_op jit(solution)/shard_map/cond/branch_1_fun/step_bit_1/pallas_call | solution.py:461
  47.1 2.0 %store.4 = (bf16[1,192,512]{2,1,0:T(8,128)(2,1)}, bf16[1,192,4096]{2,1,0:T(8,128)(2,1)}, f32[1,1024,512]{2,1,0:T(8,128)}) custom-call(bf16[1,192,512]{2,1,0:T(8,128)(2,1)S(1)} %get-tuple-element.35.proj_ref, bf16[1,192,4096]{2,1,0:T(8,128)(2,1)S(1)} %get-tuple-element.36.ig_ref, f32[1,1024,512]{2,1,0:T(8,128)S(1)} %get-tuple-element.37.mixed_ref), custom_call_target="tpu_custom_call" | custom-call | tf_op jit(solution)/shard_map/cond/branch_1_fun/store/pallas_call | solution.py:477

commit v2 on v1

--- a/solution.py
+++ b/solution.py
@@ -174,17 +174,20 @@
     wait_cot(1)
     update(chunks[0], halves[1])
 
+    busy = min(2, len(chunks) - 1)
     for c in range(1, len(chunks)):
         wait_act(c)
         send_next()
         update(chunks[c], pl.ds(0, width))
-        if c == 1:
+        if c == busy:
             for slot in order + [0]:
                 input_grad(slot)
             send_ig(1)
             later += [functools.partial(send_ig, slot) for slot in far]
-            project(0)
-        project(c)
+            for before in range(c):
+                project(before)
+        if c >= busy:
+            project(c)
     send_next(len(later))
 
     sib_copies = []
@@ -225,7 +228,7 @@
 
 
 def pair_kernel(
-    bit, half_rows, scale,
+    bit, half_rows, chunks, scale,
     step_ref, act_hbm, w_hbm, cot_hbm,
     proj_ref, ig_ref, mixed_ref,
     act, cot, w, ws, acc, p_out, p_in, q, pair_out, pair_in, w_in, s_out, s_in,
@@ -258,8 +261,11 @@
     def part(start, count):
         return pl.ds(pl.multiple_of(start, 16), count)
 
-    def lanes(slot, k):
-        return pl.ds(pl.multiple_of(owners[slot] * rows + k * size, 128), size)
+    def lanes(slot, here):
+        return pl.ds(pl.multiple_of(owners[slot] * rows + here.start, 128), here.size)
+
+    def rows_of(slot, here):
+        return pl.ds(slot * rows + here.start, here.size)
 
     load_w = pltpu.make_async_copy(w_hbm.at[0], w, local_sem.at[0])
     load_cot = pltpu.make_async_copy(cot_hbm.at[0], cot, local_sem.at[1])
@@ -275,68 +281,83 @@
     ws[pl.ds(0, rows), :] = w[...].astype(BF16)
     pl.semaphore_wait(barrier, 3)
 
+    w_copies = {}
+
     def send_w(slot, k):
         source = 2 if slot == 3 else 0
+        w_copies[slot, k] = go(
+            ws.at[rows_of(source, chunks[k])], ws.at[rows_of(slot, chunks[k])],
+            ws_send, ws_recv, slot * len(chunks) + k, far_id if slot == 2 else core_id)
+
+    def send_w_pair(j):
         return go(
-            ws.at[pl.ds(source * rows + k * size, size)], ws.at[pl.ds(slot * rows + k * size, size)],
-            ws_send, ws_recv, slot * 4 + k, far_id if slot == 2 else core_id)
-
-    w_copies = {(2, k): send_w(2, k) for k in (0, 1)}
-    w_pair = go(ws.at[part(theirs, half_rows)], w_in, pair_send, pair_recv, 0, pair_id)
+            ws.at[part(theirs + j * sub, sub)], w_in.at[pl.ds(j * sub, sub)],
+            pair_send, pair_recv, 7 + j, pair_id)
+
+    send_w(2, 0)
+    w_pair = [send_w_pair(0)]
     load_cot.wait()
     load_act.wait()
 
     def term(slot, k):
         return lax.dot_general(
-            act[:, lanes(slot, k)], cot[...], (((0,), (0,)), ((), ())), preferred_element_type=F32)
-
-    p_copies = {}
-    for k in range(4):
-        for at, slot in ((1, 3), (0, 1)):
+            act[:, lanes(slot, pl.ds(k * size, size))], cot[...],
+            (((0,), (0,)), ((), ())), preferred_element_type=F32)
+
+    def send_terms(at, slot):
+        copies = []
+        for k in range(4):
             here = pl.ds(at * rows + k * size, size)
             p_out[here, :] = term(slot, k).astype(BF16)
-            p_copies[at, k] = go(p_out.at[here], p_in.at[here], p_send, p_recv, at * 4 + k, core_id)
-    for k in range(4):
-        w_copies[1, k] = send_w(1, k)
-    for k in range(4):
-        for at, slot in ((1, 2), (0, 0)):
+            copies.append(go(p_out.at[here], p_in.at[here], p_send, p_recv, at * 4 + k, core_id))
+        return copies
+
+    def add_terms(at, slot, copies):
+        for k in range(4):
             here = pl.ds(at * rows + k * size, size)
             own = term(slot, k)
-            p_copies[at, k].wait_recv()
+            copies[k].wait_recv()
             q[here, :] = own + p_in[here, :].astype(F32)
 
     pair_copies = {}
-    for at in (1, 0):
-        for j in range(2):
-            here = pl.ds(at * half_rows + j * sub, sub)
-            pair_out[here, :] = q[part(at * rows + theirs + j * sub, sub), :].astype(BF16)
-            pair_copies[at, j] = go(
-                pair_out.at[here], pair_in.at[here], pair_send, pair_recv, 1 + at * 2 + j, pair_id)
+
+    def send_pair(at, j):
+        here = pl.ds(at * half_rows + j * sub, sub)
+        pair_out[here, :] = q[part(at * rows + theirs + j * sub, sub), :].astype(BF16)
+        pair_copies[at, j] = go(
+            pair_out.at[here], pair_in.at[here], pair_send, pair_recv, at * 2 + j, pair_id)
+
+    add_terms(1, 2, send_terms(1, 3))
+    send_pair(1, 0)
+    send_pair(1, 1)
     plain_out[...] = q[pl.ds(rows + 2 * half_rows, rows - 2 * half_rows), :].astype(BF16)
     plain_copy = go(plain_out, plain_in, far_send, far_recv, 0, far_id)
+    near = send_terms(0, 1)
+    for k in range(len(chunks)):
+        send_w(1, k)
+    add_terms(0, 0, near)
 
     step = jnp.full((1, width), step_ref[0], jnp.int32).astype(F32)
     rate = 0.3 / jnp.sqrt(1.0 + step / 50.0) * scale
 
     def multiply(slot, k):
-        block = ws[pl.ds(slot * rows + k * size, size), :]
-        ig_ref[0, :, lanes(slot, k)] = (lax.dot_general(
+        block = ws[rows_of(slot, chunks[k]), :]
+        across = lanes(slot, chunks[k])
+        ig_ref[0, :, across] = (lax.dot_general(
             cot[...], block, (((1,), (1,)), ((), ())), preferred_element_type=F32) * scale).astype(BF16)
-        out = jnp.dot(act[:, lanes(slot, k)], block, preferred_element_type=F32)
+        out = jnp.dot(act[:, across], block, preferred_element_type=F32)
         acc[...] = out if (slot, k) == (0, 0) else acc[...] + out
 
     def arrive(k):
         w_copies[2, k].wait_recv()
-        w_copies[3, k] = send_w(3, k)
-
-    for k in range(4):
-        multiply(0, k)
-    arrive(0)
-    w_copies[2, 2] = send_w(2, 2)
-    for k in range(4):
-        w_copies[1, k].wait_recv()
-        multiply(1, k)
-
+        send_w(3, k)
+
+    def forwarded(k):
+        w_copies[3, k].wait_recv()
+        multiply(3, k)
+
+    last = len(chunks) - 1
+    multiply(0, 0)
     far_copies = []
     for j in range(2):
         here = pl.ds(j * sub, sub)
@@ -345,49 +366,56 @@
             q[part(rows + mine + j * sub, sub), :] + pair_in[pl.ds(half_rows + j * sub, sub), :].astype(F32)
         ).astype(BF16)
         far_copies.append(go(s_out.at[here], s_in.at[here], far_send, far_recv, 1 + j, far_id))
-
-    arrive(1)
-    w_copies[2, 3] = send_w(2, 3)
+        send_pair(0, j)
+    w_pair.append(send_w_pair(1))
+    send_w(2, 1)
+    arrive(0)
+    for k in range(1, len(chunks)):
+        multiply(0, k)
     multiply(2, 0)
-    multiply(2, 1)
 
     plain_copy.wait_recv()
+    send_w(2, 2)
     new = w[plain, :] - rate * (q[plain, :] + plain_in[...].astype(F32))
     mixed_ref[0, plain, :] = new
     new_out[...] = new.astype(BF16)
-    new_copy = go(new_out, new_in, pair_send, pair_recv, 5, pair_id)
-
-    w_pair.wait_recv()
+    new_copy = go(new_out, new_in, pair_send, pair_recv, 4, pair_id)
+    for k in range(len(chunks)):
+        w_copies[1, k].wait_recv()
+        multiply(1, k)
+    forwarded(0)
+
     back_copies = []
     for j in range(2):
         here = pl.ds(j * sub, sub)
         there = part(mine + j * sub, sub)
+        w_pair[j].wait_recv()
         pair_copies[0, j].wait_recv()
         far_copies[j].wait_recv()
+        if j == 0:
+            for k in range(3, len(chunks)):
+                send_w(2, k)
         grad = (q[there, :] + pair_in[here, :].astype(F32)) + s_in[here, :].astype(F32)
         mean = 0.5 * ((w[there, :] + w_in[here, :].astype(F32)) - rate * grad)
         mixed_ref[0, there, :] = mean
         back_out[here, :] = mean.astype(BF16)
-        back_copies.append(go(back_out.at[here], back_in.at[here], pair_send, pair_recv, 6 + j, pair_id))
-
-    arrive(2)
-    multiply(2, 2)
-    for k in (0, 1):
-        w_copies[3, k].wait_recv()
-        multiply(3, k)
-    arrive(3)
-    multiply(2, 3)
-    w_copies[3, 2].wait_recv()
-    multiply(3, 2)
-
+        back_copies.append(go(back_out.at[here], back_in.at[here], pair_send, pair_recv, 5 + j, pair_id))
+
+    for k in range(1, last):
+        arrive(k)
+        multiply(2, k)
+        if k > 1:
+            forwarded(k - 1)
     new_copy.wait_recv()
     mixed_ref[0, plain, :] = 0.5 * (mixed_ref[0, plain, :] + new_in[...].astype(F32))
-    w_copies[3, 3].wait_recv()
-    multiply(3, 3)
-    proj_ref[0] = (acc[...] * scale).astype(BF16)
+    arrive(last)
+    forwarded(last - 1)
+    multiply(2, last)
     for j in range(2):
         back_copies[j].wait_recv()
         mixed_ref[0, part(theirs + j * sub, sub), :] = back_in[pl.ds(j * sub, sub), :].astype(F32)
+    forwarded(last)
+    proj_ref[0] = (acc[...] * scale).astype(BF16)
     for copy in started:
         copy.wait_send()
 
@@ -418,7 +446,9 @@
     in_vmem = pl.BlockSpec(memory_space=pltpu.VMEM)
     half_rows = rows * 5 // 16
     if chips == 2 and bit < 2 and rows % 1024 == 0:
-        run = functools.partial(pair_kernel, bit, half_rows, features ** (-0.5))
+        part = rows // 8
+        blocks = [pl.ds(2 * k * part, 2 * part) for k in range(3)] + [pl.ds(k * part, part) for k in (6, 7)]
+        run = functools.partial(pair_kernel, bit, half_rows, blocks, features ** (-0.5))
 
         def block(count):
             return pltpu.VMEM((count, width), BF16)
@@ -432,8 +462,8 @@
             block(rows - 2 * half_rows), block(rows - 2 * half_rows),
             block(rows - 2 * half_rows), block(rows - 2 * half_rows),
             block(half_rows), block(half_rows),
-            dma((3,)), dma((16,)), dma((16,)), dma((8,)), dma((8,)),
-            dma((3,)), dma((3,)), dma((8,)), dma((8,)),
+            dma((3,)), dma((4 * len(blocks),)), dma((4 * len(blocks),)), dma((8,)), dma((8,)),
+            dma((3,)), dma((3,)), dma((9,)), dma((9,)),
         ]
     else:
         run = functools.partial(kernel, bit, chips, chunks, features ** (-0.5))

time: 50.1 us -> 49.9 us (level)
  no operation moved by 1% of the time
where the time goes in v2:
time: 49.9 us; the launch traced here: 49.4 us
  Pallas kernels  47.6 us (95%)
  between operations  1.47 us (3%)
    pallas_call x1, Pallas kernels, step_kernel(): pl.pallas_call(run, out_shape=(pltpu.VMEM((1, tokens, width), BF16), pltp...  45.7 us
    pallas_call x1, Pallas kernels, step_kernel(): pl.pallas_call(store_kernel, out_shape=tuple((jax.ShapeDtypeStruct(part.s...  1.97 us

profile of v2, /device:TPU:0, one launch (start us, length us, event | category | flops | bytes accessed | tf_op | source)
XLA Modules:
  0.0 49.4 jit_solution(4585450644315103071)
XLA Ops:
  1.3 47.9 %conditional.1 = ((bf16[1,192,512]{2,1,0:T(8,128)(2,1)}, bf16[1,192,4096]{2,1,0:T(8,128)(2,1)}, f32[1,1024,512]{2,1,0:T(8,128)})) conditional(s32[]{:T(128)} %clamp.3, (s32[1]{0:T(128)}, bf16[1,192,4096]{2,1,0:T(8,128)(2,1)}, f32[1,1024,512]{2,1,0:T(8,128)}, bf16[1,192,512]{2,1,0:T(8,128)(2,1)}) %tuple.16, (s32[1]{0:T(128)}, ...), branch_computations={%region_0.1_spmd, %region_1.2_spmd, %region_2.3_spmd} | conditional | flops 2415919104 | bytes 8388616 | solution.py:520
  1.3 45.7 %step_bit_0.1 = (bf16[1,192,512]{2,1,0:T(8,128)(2,1)S(1)}, bf16[1,192,4096]{2,1,0:T(8,128)(2,1)S(1)}, f32[1,1024,512]{2,1,0:T(8,128)S(1)}) custom-call(s32[1]{0:T(128)} %get-tuple-element.24.step_ref, bf16[1,192,4096]{2,1,0:T(8,128)(2,1)} %get-tuple-element.69.act_hbm, f32[1,1024,512]{2,1,0:T(8,128)} %get-tuple-element.72.w_hbm, ...), custom_call_target="tpu_custom_call" | custom-call | flops 2415919104 | bytes 8388608 | tf_op jit(solution)/shard_map/cond/branch_0_fun/step_bit_0/pallas_call | solution.py:491
  47.0 2.0 %store.3 = (bf16[1,192,512]{2,1,0:T(8,128)(2,1)}, bf16[1,192,4096]{2,1,0:T(8,128)(2,1)}, f32[1,1024,512]{2,1,0:T(8,128)}) custom-call(bf16[1,192,512]{2,1,0:T(8,128)(2,1)S(1)} %get-tuple-element.28.proj_ref, bf16[1,192,4096]{2,1,0:T(8,128)(2,1)S(1)} %get-tuple-element.29.ig_ref, f32[1,1024,512]{2,1,0:T(8,128)S(1)} %get-tuple-element.30.mixed_ref), custom_call_target="tpu_custom_call" | custom-call | tf_op jit(solution)/shard_map/cond/branch_0_fun/store/pallas_call | solution.py:507

commit v3 on v2

--- a/solution.py
+++ b/solution.py
@@ -15,9 +15,9 @@
 
 def kernel(
     bit, chips, chunks, scale,
-    step_ref, act_hbm, w_hbm, cot_hbm,
+    step_hbm, act_hbm, w_hbm, cot_hbm,
     proj_ref, ig_ref, mixed_ref,
-    act, cot, w, wb, ig, part, to_sib, from_sib, to_chip, from_chip, give, take,
+    act, cot, w, wb, ig, part, to_sib, from_sib, to_chip, from_chip, give, take, step_ref,
     local_sem, cot_send, cot_recv, act_send, act_recv, ig_send, ig_recv,
     sib_send, sib_recv, chip_send, chip_recv, give_sem, take_sem,
 ):
@@ -57,9 +57,11 @@
     load_cot = pltpu.make_async_copy(cot_hbm.at[0], cot.at[of(0)], local_sem.at[0])
     load_act = pltpu.make_async_copy(act_hbm.at[0, :, cols(me)], act.at[of(0)], local_sem.at[1])
     load_w = pltpu.make_async_copy(w_hbm.at[0], w, local_sem.at[2])
+    load_step = pltpu.make_async_copy(step_hbm, step_ref, local_sem.at[3])
     load_cot.start()
     load_w.start()
     load_act.start()
+    load_step.start()
 
     barrier = pltpu.get_barrier_semaphore()
     for slot in range(1, slots):
@@ -156,6 +158,7 @@
     send_act(0)
     send_cot(1)
 
+    load_step.wait()
     step = jnp.full((1, width), step_ref[0], jnp.int32).astype(F32)
     rate = 0.3 / jnp.sqrt(1.0 + step / 50.0)
     load_w.wait()
@@ -229,10 +232,10 @@
 
 def pair_kernel(
     bit, half_rows, chunks, scale,
-    step_ref, act_hbm, w_hbm, cot_hbm,
+    step_hbm, act_hbm, w_hbm, cot_hbm,
     proj_ref, ig_ref, mixed_ref,
     act, cot, w, ws, acc, p_out, p_in, q, pair_out, pair_in, w_in, s_out, s_in,
-    plain_out, plain_in, new_out, new_in, back_out, back_in,
+    plain_out, plain_in, new_out, new_in, back_out, back_in, step_ref,
     local_sem, ws_send, ws_recv, p_send, p_recv, far_send, far_recv, pair_send, pair_recv,
 ):
     rep, me = lax.axis_index("rep"), lax.axis_index("fsdp")
@@ -267,18 +270,20 @@
     def rows_of(slot, here):
         return pl.ds(slot * rows + here.start, here.size)
 
-    load_w = pltpu.make_async_copy(w_hbm.at[0], w, local_sem.at[0])
+    head, tail = chunks[0], pl.ds(chunks[0].size, rows - chunks[0].size)
+    load_head = pltpu.make_async_copy(w_hbm.at[0, head], w.at[head], local_sem.at[0])
+    load_tail = pltpu.make_async_copy(w_hbm.at[0, tail], w.at[tail], local_sem.at[4])
     load_cot = pltpu.make_async_copy(cot_hbm.at[0], cot, local_sem.at[1])
     load_act = pltpu.make_async_copy(act_hbm.at[0], act, local_sem.at[2])
-    load_w.start()
-    load_cot.start()
-    load_act.start()
+    load_step = pltpu.make_async_copy(step_hbm, step_ref, local_sem.at[3])
+    for load in (load_head, load_tail, load_cot, load_act, load_step):
+        load.start()
 
     barrier = pltpu.get_barrier_semaphore()
     for device in (core_id, far_id, pair_id):
         pl.semaphore_signal(barrier, inc=1, device_id=device, device_id_type=MESH)
-    load_w.wait()
-    ws[pl.ds(0, rows), :] = w[...].astype(BF16)
+    load_head.wait()
+    ws[head, :] = w[head, :].astype(BF16)
     pl.semaphore_wait(barrier, 3)
 
     w_copies = {}
@@ -295,6 +300,8 @@
             pair_send, pair_recv, 7 + j, pair_id)
 
     send_w(2, 0)
+    load_tail.wait()
+    ws[tail, :] = w[tail, :].astype(BF16)
     w_pair = [send_w_pair(0)]
     load_cot.wait()
     load_act.wait()
@@ -337,6 +344,7 @@
         send_w(1, k)
     add_terms(0, 0, near)
 
+    load_step.wait()
     step = jnp.full((1, width), step_ref[0], jnp.int32).astype(F32)
     rate = 0.3 / jnp.sqrt(1.0 + step / 50.0) * scale
 
@@ -422,9 +430,9 @@
 
 def store_kernel(proj_ref, ig_ref, mixed_ref, proj_hbm, ig_hbm, mixed_hbm, sem):
     copies = [pltpu.make_async_copy(proj_ref, proj_hbm, sem.at[0])]
-    for src, dst in ((ig_ref, ig_hbm), (mixed_ref, mixed_hbm)):
-        size = src.shape[1] // 4
-        for c in range(4):
+    for src, dst, count in ((ig_ref, ig_hbm, 6), (mixed_ref, mixed_hbm, 8)):
+        size = src.shape[1] // count
+        for c in range(count):
             here = pl.ds(c * size, size)
             copies.append(pltpu.make_async_copy(src.at[0, here], dst.at[0, here], sem.at[len(copies)]))
     for copy in copies:
@@ -461,8 +469,8 @@
             block(half_rows), block(half_rows),
             block(rows - 2 * half_rows), block(rows - 2 * half_rows),
             block(rows - 2 * half_rows), block(rows - 2 * half_rows),
-            block(half_rows), block(half_rows),
-            dma((3,)), dma((4 * len(blocks),)), dma((4 * len(blocks),)), dma((8,)), dma((8,)),
+            block(half_rows), block(half_rows), pltpu.SMEM((1,), jnp.int32),
+            dma((5,)), dma((4 * len(blocks),)), dma((4 * len(blocks),)), dma((8,)), dma((8,)),
             dma((3,)), dma((3,)), dma((9,)), dma((9,)),
         ]
     else:
@@ -480,7 +488,8 @@
             pltpu.VMEM((chips * tokens, width), BF16),
             pltpu.VMEM((rows, width), BF16),
             pltpu.VMEM((rows, width), BF16),
-            dma((3,)),
+            pltpu.SMEM((1,), jnp.int32),
+            dma((4,)),
             dma((2 * count,)), dma((2 * count,)),
             dma((len(chunks) * count,)), dma((len(chunks) * count,)),
             dma((count,)), dma((count,)),
@@ -495,7 +504,7 @@
             pltpu.VMEM((1, tokens, features), BF16),
             pltpu.VMEM((1, rows, width), F32),
         ),
-        in_specs=[pl.BlockSpec(memory_space=pltpu.SMEM), anywhere, anywhere, anywhere],
+        in_specs=[anywhere] * 4,
         out_specs=(in_vmem, in_vmem, in_vmem),
         scratch_shapes=scratch,
         compiler_params=pltpu.CompilerParams(
@@ -509,7 +518,7 @@
         out_shape=tuple(jax.ShapeDtypeStruct(part.shape, part.dtype) for part in results),
         in_specs=[anywhere] * 3,
         out_specs=(anywhere, anywhere, anywhere),
-        scratch_shapes=[dma((9,))],
+        scratch_shapes=[dma((15,))],
         compiler_params=pltpu.CompilerParams(vmem_limit_bytes=2 ** 20),
         name="store",
     )(*results)

time: 49.9 us -> 49.5 us (level)
  no operation moved by 1% of the time
where the time goes in v3:
time: 49.5 us; the launch traced here: 49 us
  Pallas kernels  47.3 us (96%)
  between operations  1.47 us (3%)
    pallas_call x1, Pallas kernels, step_kernel(): pl.pallas_call(run, out_shape=(pltpu.VMEM((1, tokens, width), BF16), pltp...  45.2 us
    pallas_call x1, Pallas kernels, step_kernel(): pl.pallas_call(store_kernel, out_shape=tuple((jax.ShapeDtypeStruct(part.s...  2.02 us

profile of v3, /device:TPU:0, one launch (start us, length us, event | category | flops | bytes accessed | tf_op | source)
XLA Modules:
  0.0 49.0 jit_solution(5101116787693698042)
XLA Ops:
  1.3 47.5 %conditional.1 = ((bf16[1,192,512]{2,1,0:T(8,128)(2,1)}, bf16[1,192,4096]{2,1,0:T(8,128)(2,1)}, f32[1,1024,512]{2,1,0:T(8,128)})) conditional(s32[]{:T(128)} %clamp.3, (s32[1]{0:T(128)}, bf16[1,192,4096]{2,1,0:T(8,128)(2,1)}, f32[1,1024,512]{2,1,0:T(8,128)}, bf16[1,192,512]{2,1,0:T(8,128)(2,1)}) %tuple.16, (s32[1]{0:T(128)}, ...), branch_computations={%region_0.1_spmd, %region_1.2_spmd, %region_2.3_spmd} | conditional | flops 2415919104 | bytes 8388616 | solution.py:529
  1.3 45.2 %step_bit_0.1 = (bf16[1,192,512]{2,1,0:T(8,128)(2,1)S(1)}, bf16[1,192,4096]{2,1,0:T(8,128)(2,1)S(1)}, f32[1,1024,512]{2,1,0:T(8,128)S(1)}) custom-call(s32[1]{0:T(128)} %get-tuple-element.24.step_hbm, bf16[1,192,4096]{2,1,0:T(8,128)(2,1)} %get-tuple-element.69.act_hbm, f32[1,1024,512]{2,1,0:T(8,128)} %get-tuple-element.72.w_hbm, ...), custom_call_target="tpu_custom_call" | custom-call | flops 2415919104 | bytes 8388608 | tf_op jit(solution)/shard_map/cond/branch_0_fun/step_bit_0/pallas_call | solution.py:500
  46.5 2.0 %store.3 = (bf16[1,192,512]{2,1,0:T(8,128)(2,1)}, bf16[1,192,4096]{2,1,0:T(8,128)(2,1)}, f32[1,1024,512]{2,1,0:T(8,128)}) custom-call(bf16[1,192,512]{2,1,0:T(8,128)(2,1)S(1)} %get-tuple-element.28.proj_ref, bf16[1,192,4096]{2,1,0:T(8,128)(2,1)S(1)} %get-tuple-element.29.ig_ref, f32[1,1024,512]{2,1,0:T(8,128)S(1)} %get-tuple-element.30.mixed_ref), custom_call_target="tpu_custom_call" | custom-call | tf_op jit(solution)/shard_map/cond/branch_0_fun/store/pallas_call | solution.py:516

commit v4 on v3

--- a/solution.py
+++ b/solution.py
@@ -430,7 +430,7 @@
 
 def store_kernel(proj_ref, ig_ref, mixed_ref, proj_hbm, ig_hbm, mixed_hbm, sem):
     copies = [pltpu.make_async_copy(proj_ref, proj_hbm, sem.at[0])]
-    for src, dst, count in ((ig_ref, ig_hbm, 6), (mixed_ref, mixed_hbm, 8)):
+    for src, dst, count in ((ig_ref, ig_hbm, 4), (mixed_ref, mixed_hbm, 4)):
         size = src.shape[1] // count
         for c in range(count):
             here = pl.ds(c * size, size)
@@ -452,7 +452,7 @@
     dma = pltpu.SemaphoreType.DMA
     anywhere = pl.BlockSpec(memory_space=pl.ANY)
     in_vmem = pl.BlockSpec(memory_space=pltpu.VMEM)
-    half_rows = rows * 5 // 16
+    half_rows = rows * 11 // 32
     if chips == 2 and bit < 2 and rows % 1024 == 0:
         part = rows // 8
         blocks = [pl.ds(2 * k * part, 2 * part) for k in range(3)] + [pl.ds(k * part, part) for k in (6, 7)]
@@ -518,7 +518,7 @@
         out_shape=tuple(jax.ShapeDtypeStruct(part.shape, part.dtype) for part in results),
         in_specs=[anywhere] * 3,
         out_specs=(anywhere, anywhere, anywhere),
-        scratch_shapes=[dma((15,))],
+        scratch_shapes=[dma((9,))],
         compiler_params=pltpu.CompilerParams(vmem_limit_bytes=2 ** 20),
         name="store",
     )(*results)

time: 49.5 us -> 48.8 us (0.986)
  no operation moved by 1% of the time
where the time goes in v4:
time: 48.8 us; the launch traced here: 48.6 us
  Pallas kernels  46.9 us (96%)
  between operations  1.47 us (3%)
    pallas_call x1, Pallas kernels, step_kernel(): pl.pallas_call(run, out_shape=(pltpu.VMEM((1, tokens, width), BF16), pltp...  44.9 us
    pallas_call x1, Pallas kernels, step_kernel(): pl.pallas_call(store_kernel, out_shape=tuple((jax.ShapeDtypeStruct(part.s...  1.97 us

profile of v4, /device:TPU:0, one launch (start us, length us, event | category | flops | bytes accessed | tf_op | source)
XLA Modules:
  0.0 48.6 jit_solution(10145698947879304663)
XLA Ops:
  1.3 47.1 %conditional.1 = ((bf16[1,192,512]{2,1,0:T(8,128)(2,1)}, bf16[1,192,4096]{2,1,0:T(8,128)(2,1)}, f32[1,1024,512]{2,1,0:T(8,128)})) conditional(s32[]{:T(128)} %clamp.3, (s32[1]{0:T(128)}, bf16[1,192,4096]{2,1,0:T(8,128)(2,1)}, f32[1,1024,512]{2,1,0:T(8,128)}, bf16[1,192,512]{2,1,0:T(8,128)(2,1)}) %tuple.16, (s32[1]{0:T(128)}, ...), branch_computations={%region_0.1_spmd, %region_1.2_spmd, %region_2.3_spmd} | conditional | flops 2415919104 | bytes 8388616 | solution.py:529
  1.3 44.9 %step_bit_0.1 = (bf16[1,192,512]{2,1,0:T(8,128)(2,1)S(1)}, bf16[1,192,4096]{2,1,0:T(8,128)(2,1)S(1)}, f32[1,1024,512]{2,1,0:T(8,128)S(1)}) custom-call(s32[1]{0:T(128)} %get-tuple-element.24.step_hbm, bf16[1,192,4096]{2,1,0:T(8,128)(2,1)} %get-tuple-element.69.act_hbm, f32[1,1024,512]{2,1,0:T(8,128)} %get-tuple-element.72.w_hbm, ...), custom_call_target="tpu_custom_call" | custom-call | flops 2415919104 | bytes 8388608 | tf_op jit(solution)/shard_map/cond/branch_0_fun/step_bit_0/pallas_call | solution.py:500
  46.2 2.0 %store.3 = (bf16[1,192,512]{2,1,0:T(8,128)(2,1)}, bf16[1,192,4096]{2,1,0:T(8,128)(2,1)}, f32[1,1024,512]{2,1,0:T(8,128)}) custom-call(bf16[1,192,512]{2,1,0:T(8,128)(2,1)S(1)} %get-tuple-element.28.proj_ref, bf16[1,192,4096]{2,1,0:T(8,128)(2,1)S(1)} %get-tuple-element.29.ig_ref, f32[1,1024,512]{2,1,0:T(8,128)S(1)} %get-tuple-element.30.mixed_ref), custom_call_target="tpu_custom_call" | custom-call | tf_op jit(solution)/shard_map/cond/branch_0_fun/store/pallas_call | solution.py:516

commit v5 on v4

--- a/solution.py
+++ b/solution.py
@@ -72,24 +72,24 @@
     far = list(range(2, slots))
     order = far + [1]
     width = w.shape[1]
-    halves = [pl.ds(0, width // 2), pl.ds(width // 2, width // 2)]
+    spans = [pl.ds(0, width // 4), pl.ds(width // 4, width // 4), pl.ds(width // 2, width // 2)]
     cot_copies, act_copies, ig_copies = {}, {}, {}
 
     def start_cot(h, src, slot, peer):
         copy = to_peer(
-            src, cot.at[of(slot), halves[h]],
+            src, cot.at[of(slot), spans[h]],
             cot_send.at[h * slots + slot], cot_recv.at[h * slots + slot], peer)
         copy.start()
         cot_copies[h, slot] = copy
 
     def send_cot(h):
         for slot in list(range(2, slots, 2)) + [1]:
-            start_cot(h, cot_hbm.at[0, :, halves[h]], slot, receiver(slot))
+            start_cot(h, cot_hbm.at[0, :, spans[h]], slot, receiver(slot))
 
     def take_cot(h):
         for slot in range(2, slots, 2):
             cot_copies[h, slot].wait_recv()
-            start_cot(h, cot.at[of(slot), halves[h]], slot + 1, device(0, 1))
+            start_cot(h, cot.at[of(slot), spans[h]], slot + 1, device(0, 1))
 
     def wait_cot(h):
         for slot in range(1, slots, 2):
@@ -157,6 +157,7 @@
     send_cot(0)
     send_act(0)
     send_cot(1)
+    send_cot(2)
 
     load_step.wait()
     step = jnp.full((1, width), step_ref[0], jnp.int32).astype(F32)
@@ -170,12 +171,15 @@
     wait_cot(0)
     wait_act(0)
     send_next()
-    update(chunks[0], halves[0])
+    update(chunks[0], spans[0])
     take_cot(1)
+    wait_cot(1)
+    update(chunks[0], spans[1])
+    take_cot(2)
     send_next()
     wb[...] = w[...].astype(BF16)
-    wait_cot(1)
-    update(chunks[0], halves[1])
+    wait_cot(2)
+    update(chunks[0], spans[2])
 
     busy = min(2, len(chunks) - 1)
     for c in range(1, len(chunks)):
@@ -447,7 +451,7 @@
     chips = count // 2
     chunks = [pl.ds(start, 128) for start in range(0, min(rows, 256), 128)]
     chunks += [pl.ds(start, 256) for start in range(256, rows, 256)]
-    pieces = len(chunks) + 1
+    pieces = len(chunks) + 2
     every = count * tokens
     dma = pltpu.SemaphoreType.DMA
     anywhere = pl.BlockSpec(memory_space=pl.ANY)
@@ -490,7 +494,7 @@
             pltpu.VMEM((rows, width), BF16),
             pltpu.SMEM((1,), jnp.int32),
             dma((4,)),
-            dma((2 * count,)), dma((2 * count,)),
+            dma((3 * count,)), dma((3 * count,)),
             dma((len(chunks) * count,)), dma((len(chunks) * count,)),
             dma((count,)), dma((count,)),
             dma((chips,)), dma((chips,)),

time: 48.8 us -> 48.9 us (level)
  no operation moved by 1% of the time
where the time goes in v5:
time: 48.9 us
  Pallas kernels  47 us (96%)
  between operations  1.47 us (3%)
    pallas_call x1, Pallas kernels, step_kernel(): pl.pallas_call(run, out_shape=(pltpu.VMEM((1, tokens, width), BF16), pltp...  45 us
    pallas_call x1, Pallas kernels, step_kernel(): pl.pallas_call(store_kernel, out_shape=tuple((jax.ShapeDtypeStruct(part.s...  1.97 us

profile of v5, /device:TPU:0, one launch (start us, length us, event | category | flops | bytes accessed | tf_op | source)
XLA Modules:
  0.0 48.9 jit_solution(12154447243689092377)
XLA Ops:
  1.3 47.4 %conditional.1 = ((bf16[1,192,512]{2,1,0:T(8,128)(2,1)}, bf16[1,192,4096]{2,1,0:T(8,128)(2,1)}, f32[1,1024,512]{2,1,0:T(8,128)})) conditional(s32[]{:T(128)} %clamp.3, (s32[1]{0:T(128)}, bf16[1,192,4096]{2,1,0:T(8,128)(2,1)}, f32[1,1024,512]{2,1,0:T(8,128)}, bf16[1,192,512]{2,1,0:T(8,128)(2,1)}) %tuple.16, (s32[1]{0:T(128)}, ...), branch_computations={%region_0.1_spmd, %region_1.2_spmd, %region_2.3_spmd} | conditional | flops 2415919104 | bytes 8388616 | solution.py:533
  1.3 45.0 %step_bit_1.1 = (bf16[1,192,512]{2,1,0:T(8,128)(2,1)S(1)}, bf16[1,192,4096]{2,1,0:T(8,128)(2,1)S(1)}, f32[1,1024,512]{2,1,0:T(8,128)S(1)}) custom-call(s32[1]{0:T(128)} %get-tuple-element.31.step_hbm, bf16[1,192,4096]{2,1,0:T(8,128)(2,1)} %get-tuple-element.70.act_hbm, f32[1,1024,512]{2,1,0:T(8,128)} %get-tuple-element.73.w_hbm, ...), custom_call_target="tpu_custom_call" | custom-call | flops 2415919104 | bytes 8388608 | tf_op jit(solution)/shard_map/cond/branch_1_fun/step_bit_1/pallas_call | solution.py:504
  46.3 2.0 %store.4 = (bf16[1,192,512]{2,1,0:T(8,128)(2,1)}, bf16[1,192,4096]{2,1,0:T(8,128)(2,1)}, f32[1,1024,512]{2,1,0:T(8,128)}) custom-call(bf16[1,192,512]{2,1,0:T(8,128)(2,1)S(1)} %get-tuple-element.35.proj_ref, bf16[1,192,4096]{2,1,0:T(8,128)(2,1)S(1)} %get-tuple-element.36.ig_ref, f32[1,1024,512]{2,1,0:T(8,128)S(1)} %get-tuple-element.37.mixed_ref), custom_call_target="tpu_custom_call" | custom-call | tf_op jit(solution)/shard_map/cond/branch_1_fun/store/pallas_call | solution.py:520
